TPU v7x, 32 devices: a whole 2x2x4 slice. The times are simulated.
32 devices in a mesh: groups: 2 (over y), expert: 4 (over x, core), tensor: 4 (over z).
Axes of the slice: x: 2, y: 2, z: 4, core: 2. Of those that a mesh axis runs over, the one named last changes fastest.
Arguments:
- tokens: bfloat16 [1024, 6144], P(('groups', 'expert'), 'tensor'), parts along dimension 0, may hold values from -6 to 6
- routes: int32 [1024, 2], P(('groups', 'expert')), parts along dimension 0, may hold values from 0 to 3, all different within a row; in each aligned block of 128 rows (0 to 127, 128 to 255, ...) at most 72 rows name the same one
- route_weights: bfloat16 [1024, 2], P(('groups', 'expert')), parts along dimension 0, may hold values from 0.099609375 to 1
- gate_weight: bfloat16 [6144, 32768], P(None, ('expert', 'tensor')), may hold values from -0.078125 to 0.078125
- up_weight: bfloat16 [6144, 32768], P(None, ('expert', 'tensor')), may hold values from -0.078125 to 0.078125
- down_weight: bfloat16 [32768, 6144], P(('expert', 'tensor')), may hold values from -0.0625 to 0.0625
Outputs:
- mixed: bfloat16 [1024, 6144], P(('groups', 'expert'), 'tensor'), parts along dimension 0
There are 2 independent parts, one for each index of `groups`. A program takes and returns all parts, laid end to end along the dimension named above; an argument that names none is the same for every part. Nothing has to cross between parts.
Inputs may be any that keep to these rules, and one draw needn't show every extreme that they name: `routes`: each row names 2 different experts. In each aligned block of 128 rows (the tokens of one index of the expert axis) no expert is named by more than 72 rows, a bound that some block reaches.
All inputs are finite; a program needn't handle non-finite values.
Results may differ from a plain program's by a relative error of at most 0.013.
Values may be sent and summed in bfloat16 or wider, within the bound.
A program may use at most 192 MiB of HBM per device.

v0:
```python
import jax
import jax.numpy as jnp
from jax import lax
from jax.sharding import PartitionSpec as P

EXPERTS = 4
TOP = 2
CAP = 72


def assign(flat, targets, capacity):
    hit = (flat[:, None, :] == targets[:, :, None]).astype(jnp.int32)
    rank = jnp.cumsum(hit, axis=2) - hit
    slots = lax.broadcasted_iota(jnp.int32, (1, 1, capacity, 1), 2)
    picked = (rank[:, :, None, :] == slots) & (hit[:, :, None, :] == 1)
    return picked.astype(jnp.float32)


def split_parts(values):
    upper = values.astype(jnp.bfloat16)
    lower = (values - upper.astype(jnp.float32)).astype(jnp.bfloat16)
    return (upper, lower)


def per_device(tokens, routes, route_weights, gate_weight, up_weight, down_weight):
    expert_count = lax.axis_size("expert")
    copies = expert_count // EXPERTS
    tok_count = tokens.shape[0]
    local_width = tokens.shape[1]
    features = lax.all_gather(tokens, "tensor", axis=1, tiled=True)
    width = features.shape[1]
    flat = routes.reshape(1, -1)
    targets = lax.broadcasted_iota(jnp.int32, (1, EXPERTS), 1)
    table = assign(flat, targets, CAP)[0]
    doubled = jnp.repeat(features, TOP, axis=0)
    packed = jnp.einsum(
        "ecq,qd->ecd", table.astype(jnp.bfloat16), doubled, preferred_element_type=jnp.float32
    ).astype(jnp.bfloat16)
    outgoing = jnp.broadcast_to(packed[:, None], (EXPERTS, copies, CAP, width)).reshape(
        expert_count, CAP, width
    )
    incoming = lax.all_to_all(outgoing, "expert", split_axis=0, concat_axis=0, tiled=True)
    received = incoming.reshape(expert_count * CAP, width)
    gate = jnp.dot(received, gate_weight, preferred_element_type=jnp.float32)
    up = jnp.dot(received, up_weight, preferred_element_type=jnp.float32)
    hidden = (jax.nn.silu(gate) * up).astype(jnp.bfloat16)
    partial_rows = lax.psum_scatter(
        lax.dot_general(
            down_weight, hidden, (((0,), (1,)), ((), ())), preferred_element_type=jnp.float32
        ).astype(jnp.bfloat16),
        "tensor",
        scatter_dimension=0,
        tiled=True,
    ).astype(jnp.float32)
    returned = lax.all_to_all(
        partial_rows.astype(jnp.bfloat16), "expert", split_axis=1, concat_axis=1, tiled=True
    ).astype(partial_rows.dtype)
    summed = (
        returned.reshape(local_width, EXPERTS, copies, CAP)
        .sum(axis=2)
        .reshape(local_width, EXPERTS * CAP)
    )
    selector = table.reshape(EXPERTS * CAP, -1).astype(jnp.bfloat16)
    upper, lower = split_parts(summed)
    gathered = jnp.dot(upper, selector, preferred_element_type=jnp.float32) + jnp.dot(
        lower, selector, preferred_element_type=jnp.float32
    )
    scales = route_weights.astype(jnp.float32).reshape(1, -1)
    result = (gathered * scales).reshape(local_width, tok_count, TOP).sum(axis=2)
    return result.T.astype(jnp.bfloat16)


def solution(mesh):
    in_specs = (
        P(("groups", "expert"), "tensor"),
        P(("groups", "expert"), None),
        P(("groups", "expert"), None),
        P(None, ("expert", "tensor")),
        P(None, ("expert", "tensor")),
        P(("expert", "tensor"), None),
    )
    out_specs = P(("groups", "expert"), "tensor")
    return jax.shard_map(
        per_device, mesh=mesh, in_specs=in_specs, out_specs=out_specs, check_vma=False
    )
```

profile of v0, /device:TPU:0, one launch (start us, length us, event | category | flops | bytes accessed | tf_op | source)
XLA Modules:
  0.0 233.7 jit_solution(10942101690418543534)
XLA Ops:
  6.5 0.0 all-gather.2.cloned.1.call-start
  6.5 0.7 all-gather.2.cloned.1.call-update
  7.3 0.0 reduce-scatter.2.cloned.1.call-start
  7.3 0.8 copy.9
  8.1 0.1 eq.71
  8.2 0.1 eq.75
  8.4 1.2 reduce-window.6
  9.6 0.1 slice.8
  9.7 0.1 copy.10
  9.8 0.1 copy.11
  9.9 0.1 broadcast_bitcast_fusion
  10.0 38.7 %all-gather.2.cloned.1.call-done = bf16[128,6144]{1,0:T(8,128)(2,1)} async-done(((bf16[128,1536]{1,0:T(8,128)(2,1)}), bf16[128,6144]{1,0:T(8,128)(2,1)}) %all-gather.2.cloned.1.call-update) | async-done | bytes 1572880 | tf_op jit(solution)/shard_map/all_gather | solution.py:30
  48.8 3.3 %broadcast_in_dim.2 = bf16[128,2,6144]{2,1,0:T(2,128)(2,1)S(1)} broadcast(bf16[128,6144]{1,0:T(8,128)(2,1)} %all-gather.2.cloned.1.call-done), dimensions={0,2} | broadcast | bytes 4718592 | tf_op jit(solution)/shard_map/broadcast_in_dim | solution.py:35
  52.1 2.7 %reshape.163 = bf16[256,6144,1]{1,0,2:T(8,128)(2,1)} reshape(bf16[128,2,6144]{2,1,0:T(2,128)(2,1)S(1)} %broadcast_in_dim.2) | data formatting | bytes 6291456 | tf_op jit(solution)/shard_map/reshape | solution.py:35
  54.8 3.0 %convolution_convert_fusion.1 = bf16[4,72,6144]{2,1,0:T(8,128)(2,1)S(1)} fusion(bf16[256,6144,1]{1,0,2:T(8,128)(2,1)} %reshape.163, s32[4,256]{1,0:T(4,128)S(1)} %convert_subtract_fusion, pred[4,256]{1,0:T(4,128)(4,1)S(1)} %convert_compare_fusion), kind=kOutput, calls=%fused_computation.1 | convolution fusion | flops 908034048 | bytes 6689792 | tf_op jit(solution)/shard_map/ecq,qd->ecd/dot_general | solution.py:36
  57.8 43.7 %all_to_all.14 = bf16[4,72,6144]{2,1,0:T(8,128)(2,1)S(1)} all-to-all(bf16[4,72,6144]{2,1,0:T(8,128)(2,1)S(1)} %convolution_convert_fusion.1), channel_id=1, replica_groups=mesh['groups'=2,'expert'=4,'tensor'=4] {'expert'}, dimensions={0} | all-to-all | bytes 7077888 | tf_op jit(solution)/shard_map/all_to_all | solution.py:42
  101.5 13.4 %fusion.18 = f32[288,2048]{1,0:T(8,128)} fusion(bf16[288,6144]{1,0:T(8,128)(2,1)S(1)} %bitcast.37, bf16[6144,2048]{1,0:T(8,128)(2,1)} %param.9), kind=kOutput, calls=%fused_computation.34 | convolution fusion | flops 7247757312 | bytes 31064064 | tf_op jit(solution)/shard_map/dot_general | solution.py:44
  114.9 23.9 %fusion = bf16[6144,288]{0,1:T(8,128)(2,1)} fusion(bf16[2048,6144]{1,0:T(8,128)(2,1)} %param.11, bf16[288,6144]{1,0:T(8,128)(2,1)S(1)} %bitcast.38, bf16[6144,2048]{1,0:T(8,128)(2,1)} %param.10, f32[288,2048]{1,0:T(8,128)} %fusion.18), kind=kOutput, calls=%fused_computation.2 | convolution fusion | flops 14500823040 | bytes 59768832 | tf_op jit(solution)/shard_map/dot_general | solution.py:48
  138.8 0.0 copy-start
  138.8 0.0 reduce-scatter.2.cloned.1.call-update
  138.8 64.5 %reduce-scatter.2.cloned.1.call-done = bf16[1536,288]{0,1:T(8,128)(2,1)} async-done(((bf16[6144,288]{0,1:T(8,128)(2,1)}), bf16[1536,288]{0,1:T(8,128)(2,1)}) %reduce-scatter.2.cloned.1.call-update) | async-done | bytes 884752 | tf_op jit(solution)/shard_map/reduce_scatter | solution.py:47
  203.3 3.7 %all-to-all-start.1 = ((bf16[1536,4,72]{0,2,1:T(8,128)(2,1)}), bf16[1536,4,72]{0,2,1:T(8,128)(2,1)S(1)}, u32[]{:S(2)}, u32[]{:S(2)}) async-start(bf16[1536,4,72]{0,2,1:T(8,128)(2,1)} %bitcast.39), calls=%async_computation.2 | async-start | bytes 1769472 | tf_op jit(solution)/shard_map/all_to_all | solution.py:55
  207.0 0.0 copy-done
  207.0 0.1 copy.13
  207.1 0.1 reshape.162
  207.3 12.2 %all-to-all-done.1 = bf16[1536,4,72]{0,2,1:T(8,128)(2,1)S(1)} async-done(((bf16[1536,4,72]{0,2,1:T(8,128)(2,1)}), bf16[1536,4,72]{0,2,1:T(8,128)(2,1)S(1)}, u32[]{:S(2)}, u32[]{:S(2)}) %all-to-all-start.1) | async-done | bytes 884768 | tf_op jit(solution)/shard_map/all_to_all | solution.py:55
  219.5 0.6 convolution_bitcast_fusion
  220.1 0.6 fusion.2
  220.8 2.1 reshape.161
  222.8 4.1 %reduce_sum.8 = bf16[1536,128]{0,1:T(8,128)(2,1)} reduce(f32[1536,128,2]{0,2,1:T(2,128)} %reshape.161, f32[]{:T(128)} %constant.10.clone.1), dimensions={2}, to_apply=%region_3.4 | reduce | flops 196608 | bytes 1966084 | tf_op jit(solution)/shard_map/reduce_sum | solution.py:69
  (5 shorter events, 0.1 us)
Async XLA Ops:
  6.5 42.2 %all-gather.2.cloned.1.call-start = ((), (), s32[]{:S(2)}) async-start(), calls=%async_computation.3 | async-start | bytes 1966080 | tf_op jit(solution)/shard_map/all_gather | solution.py:30
  7.3 196.1 %reduce-scatter.2.cloned.1.call-start = ((), (), s32[]{:S(2)}) async-start(), calls=%async_computation.4 | async-start | bytes 4423680 | tf_op jit(solution)/shard_map/reduce_scatter | solution.py:47
  138.8 68.2 %copy-start = (bf16[128,2]{0,1:T(2,128)(2,1)S(1)}, bf16[128,2]{0,1:T(2,128)(2,1)}, u32[]{:S(2)}) copy-start(bf16[128,2]{0,1:T(2,128)(2,1)} %param.8) | copy-start | bytes 1540
  203.3 16.2 %all-to-all-start.1 = ((bf16[1536,4,72]{0,2,1:T(8,128)(2,1)}), bf16[1536,4,72]{0,2,1:T(8,128)(2,1)S(1)}, u32[]{:S(2)}, u32[]{:S(2)}) async-start(bf16[1536,4,72]{0,2,1:T(8,128)(2,1)} %bitcast.39), calls=%async_computation.2 | async-start | bytes 1769472 | tf_op jit(solution)/shard_map/all_to_all | solution.py:55
Sparse Core Ops, SparseCore 0:
  8.9 39.7 all-gather.1
  139.0 64.3 reduce-scatter.1
where the time goes:
time: 234 us
  waiting for transfers between devices  116 us (50%)
  blocking collectives  43.7 us (19%)
  matrix products  41.6 us (18%)
  between operations  13.5 us (6%)
  local copies, waits for them, and re-layouts  9.77 us (4%)
  other arithmetic  5.34 us (2%)
  starting transfers between devices  3.72 us (2%)
    reduce_scatter x1, waiting for transfers between devices, per_device(): lax.psum_scatter(lax.dot_general(down_weight, hidden, (((0,), (1,)), ((),...  64.5 us
    all_to_all x1, blocking collectives, per_device(): lax.all_to_all(outgoing, 'expert', split_axis=0, concat_axis=0, tiled=True)  43.7 us
    all_gather x1, waiting for transfers between devices, per_device(): features = lax.all_gather(tokens, 'tensor', axis=1, tiled=True)  38.7 us
    dot_general x1, matrix products, per_device(): lax.dot_general(down_weight, hidden, (((0,), (1,)), ((), ())), preferred_...  23.9 us
    dot_general x1, matrix products, per_device(): gate = jnp.dot(received, gate_weight, preferred_element_type=jnp.float32)  13.4 us
    all_to_all x1, waiting for transfers between devices, per_device(): lax.all_to_all(partial_rows.astype(jnp.bfloat16), 'expert', split_axis=1,...  12.2 us
  transfers between devices with their start and end apart: 3, of which 3 were waited for; matrix products, arithmetic and copies ran while one was open for 1% of the time, Pallas kernels for 0%

commit v1 on v0

--- a/solution.py
+++ b/solution.py
@@ -1,12 +1,359 @@
+import functools
+
 import jax
 import jax.numpy as jnp
 from jax import lax
+from jax.experimental import pallas as pl
+from jax.experimental.pallas import tpu as pltpu
 from jax.sharding import PartitionSpec as P
 
 EXPERTS = 4
 TOP = 2
 CAP = 72
-
+BF = jnp.bfloat16
+F32 = jnp.float32
+W_SLOTS = 3
+D_SLOTS = 3
+K_SLOTS = 4
+ROLES = 4
+
+
+def kernel(
+    nt, nq, tok, meta, wg, wu, wd, out,
+    xbuf, packed, acc_g, acc_u, hid, gbuf, ubuf, dbuf, pick, spread, meta_in,
+    keep, sib_out, sib_in, x_out, x_in, z_out, z_in,
+    tok_sem, w_sem, d_sem, meta_s, meta_r,
+    zs_s, zs_r, xs_s, xs_r, own_s, own_r, fwd_s, fwd_r,
+    rsib_s, rsib_r, rx_s, rx_r, rz_s, rz_r,
+):
+    n = nt * nq
+    kc = xbuf.shape[3]
+    tokens = tok.shape[0]
+    rows = ROLES * CAP
+    z = lax.axis_index("tensor")
+    ex = lax.axis_index("expert")
+    core = lax.rem(ex, 2)
+    chip = lax.div(ex, 2)
+    sib = 2 * chip + 1 - core
+    xp = 2 * (1 - chip) + core
+    dg = 2 * (1 - chip) + 1 - core
+    my_expert = ex
+
+    def offset(d):
+        return lax.rem(z + ((d + 1) // 2) * (2 * (d % 2) - 1) + nt, nt)
+
+    def offset_t(d):
+        return lax.rem(z + lax.div(d + 1, 2) * (2 * lax.rem(d, 2) - 1) + nt, nt)
+
+    def at_expert(src, dst, s, r, who):
+        return pltpu.make_async_remote_copy(
+            src_ref=src, dst_ref=dst, send_sem=s, recv_sem=r,
+            device_id={"expert": who}, device_id_type=pl.DeviceIdType.MESH)
+
+    def at_tensor(src, dst, s, r, who):
+        return pltpu.make_async_remote_copy(
+            src_ref=src, dst_ref=dst, send_sem=s, recv_sem=r,
+            device_id={"tensor": who}, device_id_type=pl.DeviceIdType.MESH)
+
+    def tok_copy(q):
+        return pltpu.make_async_copy(
+            tok.at[:, pl.ds(q * kc, kc)], xbuf.at[z * nq + q, 0], tok_sem.at[q])
+
+    def g_copy(i, k):
+        s = lax.rem(i, W_SLOTS)
+        r = pl.ds(pl.multiple_of(k * kc, kc), kc)
+        return pltpu.make_async_copy(wg.at[r, :], gbuf.at[s], w_sem.at[0, s])
+
+    def u_copy(i, k):
+        s = lax.rem(i, W_SLOTS)
+        r = pl.ds(pl.multiple_of(k * kc, kc), kc)
+        return pltpu.make_async_copy(wu.at[r, :], ubuf.at[s], w_sem.at[1, s])
+
+    def d_copy(i, k):
+        s = lax.rem(i, D_SLOTS)
+        r = pl.ds(pl.multiple_of(k * kc, kc), kc)
+        return pltpu.make_async_copy(wd.at[:, r], dbuf.at[s], d_sem.at[s])
+
+    def in_chunk(i):
+        return offset_t(lax.rem(i, nt)) * nq + lax.div(i, nt)
+
+    def out_owner(i):
+        return offset_t(lax.rem(i + 1, nt))
+
+    def out_chunk(i):
+        return out_owner(i) * nq + lax.div(i, nt)
+
+    def z_copy(d, q):
+        s = (d - 1) * nq + q
+        k = z * nq + q
+        return at_tensor(xbuf.at[k, 0], xbuf.at[k, 0], zs_s.at[s], zs_r.at[k], offset(d))
+
+    def z_arrival(k):
+        return at_tensor(xbuf.at[k, 0], xbuf.at[k, 0], zs_s.at[0], zs_r.at[k], offset(1))
+
+    def x_copy(k):
+        return at_expert(xbuf.at[k, 0], xbuf.at[k, 1], xs_s.at[k], xs_r.at[k], xp)
+
+    def own_copy(k):
+        return at_expert(xbuf.at[k, 0], xbuf.at[k, 2], own_s.at[k], own_r.at[k], sib)
+
+    def fwd_copy(k):
+        return at_expert(xbuf.at[k, 1], xbuf.at[k, 3], fwd_s.at[k], fwd_r.at[k], sib)
+
+    def rsib_copy(k):
+        return at_expert(sib_out.at[k], sib_in.at[k], rsib_s.at[k], rsib_r.at[k], sib)
+
+    def rx_copy(k):
+        return at_expert(x_out.at[k], x_in.at[k], rx_s.at[k], rx_r.at[k], xp)
+
+    def rz_copy(k, q, who):
+        return at_tensor(z_out.at[k], z_in.at[z * nq + q], rz_s.at[k], rz_r.at[z * nq + q], who)
+
+    def rz_arrival(k):
+        return at_tensor(z_out.at[k], z_in.at[k], rz_s.at[k], rz_r.at[k], offset(1))
+
+    def meta_copy(role, who):
+        return at_expert(
+            meta.at[who], meta_in.at[role], meta_s.at[role], meta_r.at[role], who)
+
+    for q in range(nq):
+        tok_copy(q).start()
+    for i in range(W_SLOTS):
+        g_copy(i, in_chunk(i)).start()
+        u_copy(i, in_chunk(i)).start()
+
+    barrier = pltpu.get_barrier_semaphore()
+    for who in (sib, xp, dg):
+        pl.semaphore_signal(
+            barrier, inc=1, device_id={"expert": who}, device_id_type=pl.DeviceIdType.MESH)
+    for d in range(1, nt):
+        pl.semaphore_signal(
+            barrier, inc=1, device_id={"tensor": offset(d)}, device_id_type=pl.DeviceIdType.MESH)
+    pl.semaphore_wait(barrier, 3 + nt - 1)
+
+    partners = ((1, xp), (2, sib), (3, dg))
+    for role, who in partners:
+        meta_copy(role, who).start()
+    for q in range(nq):
+        tok_copy(q).wait()
+        for d in range(1, nt):
+            z_copy(d, q).start()
+        x_copy(z * nq + q).start()
+        own_copy(z * nq + q).start()
+    for i in range(D_SLOTS):
+        d_copy(i, out_chunk(i)).start()
+
+    acc_g[...] = jnp.zeros_like(acc_g)
+    acc_u[...] = jnp.zeros_like(acc_u)
+    meta_in[0] = meta[my_expert]
+    for role, who in partners:
+        meta_copy(role, who).wait_recv()
+    eye = lax.broadcasted_iota(jnp.int32, (tokens, tokens), 0) == lax.broadcasted_iota(
+        jnp.int32, (tokens, tokens), 1)
+    row_id = lax.broadcasted_iota(jnp.int32, (rows, tokens), 0).astype(F32)
+    for role in range(ROLES):
+        slot = meta_in[role, 0:1, :]
+        weight = meta_in[role, 1:2, :]
+        slot = jnp.where(slot >= 0, slot + role * CAP, -1.0)
+        hot = jnp.where(row_id == slot, 1.0, 0.0).astype(BF)
+        pick[:, role * tokens:(role + 1) * tokens] = hot
+        scale = jnp.where(eye, jnp.broadcast_to(weight, (tokens, tokens)), 0.0).astype(BF)
+        spread[role * tokens:(role + 1) * tokens, :] = lax.dot_general(
+            scale, hot, (((1,), (1,)), ((), ())), preferred_element_type=F32).astype(BF)
+
+    tile = 512 if gbuf.shape[2] % 512 == 0 else gbuf.shape[2]
+
+    def gather_step(i, carry):
+        @pl.when(i < n)
+        def _():
+            @pl.when(lax.rem(i, nt) > 0)
+            def _():
+                k = in_chunk(i)
+                z_arrival(k).wait_recv()
+                x_copy(k).start()
+                own_copy(k).start()
+
+        @pl.when((i >= 1) & (i < n + 1))
+        def _():
+            k = in_chunk(i - 1)
+            x_copy(k).wait_recv()
+            fwd_copy(k).start()
+
+        @pl.when(i >= 2)
+        def _():
+            j = i - 2
+            k = in_chunk(j)
+            s = lax.rem(j, W_SLOTS)
+            own_copy(k).wait_recv()
+            fwd_copy(k).wait_recv()
+            packed[...] = jnp.dot(
+                pick[...], xbuf[k].reshape(ROLES * tokens, kc), preferred_element_type=F32
+            ).astype(BF)
+            g_copy(j, k).wait()
+            u_copy(j, k).wait()
+
+            def column(t, c2):
+                cols = pl.ds(pl.multiple_of(t * tile, tile), tile)
+                acc_g[:, cols] += jnp.dot(packed[...], gbuf[s, :, cols], preferred_element_type=F32)
+                acc_u[:, cols] += jnp.dot(packed[...], ubuf[s, :, cols], preferred_element_type=F32)
+                return c2
+
+            lax.fori_loop(0, gbuf.shape[2] // tile, column, 0)
+
+            @pl.when(j + W_SLOTS < n)
+            def _():
+                k2 = in_chunk(j + W_SLOTS)
+                g_copy(j + W_SLOTS, k2).start()
+                u_copy(j + W_SLOTS, k2).start()
+
+        return carry
+
+    lax.fori_loop(0, n + 2, gather_step, 0)
+
+    def activate(t, carry):
+        cols = pl.ds(pl.multiple_of(t * tile, tile), tile)
+        hid[:, cols] = (jax.nn.silu(acc_g[:, cols]) * acc_u[:, cols]).astype(BF)
+        return carry
+
+    lax.fori_loop(0, gbuf.shape[2] // tile, activate, 0)
+
+    width = 256
+
+    def return_step(i, carry):
+        @pl.when(i < n)
+        def _():
+            k = out_chunk(i)
+            s = lax.rem(i, D_SLOTS)
+            ks = lax.rem(i, K_SLOTS)
+            d_copy(i, k).wait()
+
+            def column(t, c2):
+                cols = pl.ds(pl.multiple_of(t * width, width), width)
+                term = jnp.dot(hid[...], dbuf[s, :, cols], preferred_element_type=F32).astype(BF)
+                share = jnp.dot(spread[...], term, preferred_element_type=F32)
+                keep[ks, :, cols] = share[:2 * tokens]
+                sib_out[k, :, cols] = share[2 * tokens:].astype(BF)
+                return c2
+
+            lax.fori_loop(0, kc // width, column, 0)
+            rsib_copy(k).start()
+
+            @pl.when(i + D_SLOTS < n)
+            def _():
+                d_copy(i + D_SLOTS, out_chunk(i + D_SLOTS)).start()
+
+        @pl.when((i >= 1) & (i < n + 1))
+        def _():
+            k = out_chunk(i - 1)
+            ks = lax.rem(i - 1, K_SLOTS)
+            rsib_copy(k).wait_recv()
+            x_out[k] = (keep[ks, tokens:] + sib_in[k, tokens:].astype(F32)).astype(BF)
+            rx_copy(k).start()
+
+        @pl.when(i >= 2)
+        def _():
+            j = i - 2
+            k = out_chunk(j)
+            ks = lax.rem(j, K_SLOTS)
+            rx_copy(k).wait_recv()
+            z_out[k] = (
+                keep[ks, :tokens] + sib_in[k, :tokens].astype(F32) + x_in[k].astype(F32)
+            ).astype(BF)
+
+            @pl.when(lax.rem(j + 1, nt) > 0)
+            def _():
+                rz_copy(k, lax.div(j, nt), out_owner(j)).start()
+
+        return carry
+
+    lax.fori_loop(0, n + 2, return_step, 0)
+
+    for q in range(nq):
+        total = z_out[z * nq + q].astype(F32)
+        for d in range(1, nt):
+            k = offset(d) * nq + q
+            rz_arrival(k).wait_recv()
+            total = total + z_in[k].astype(F32)
+        out[:, q * kc:(q + 1) * kc] = total.astype(BF)
+
+    for role, who in partners:
+        meta_copy(role, who).wait_send()
+    for q in range(nq):
+        for d in range(1, nt):
+            z_copy(d, q).wait_send()
+
+    def drain(k, carry):
+        x_copy(k).wait_send()
+        own_copy(k).wait_send()
+        fwd_copy(k).wait_send()
+        rsib_copy(k).wait_send()
+        rx_copy(k).wait_send()
+        return carry
+
+    lax.fori_loop(0, n, drain, 0)
+    for q in range(nq):
+        for d in range(1, nt):
+            rz_copy(offset(d) * nq + q, q, offset(d)).wait_send()
+
+
+def fused(mesh, tokens, routes, route_weights, gate_weight, up_weight, down_weight):
+    nt = mesh.shape["tensor"]
+    count, local_width = tokens.shape
+    hidden = gate_weight.shape[1]
+    kc = 768
+    nq = local_width // kc
+    n = nt * nq
+    rows = ROLES * CAP
+    ids = lax.broadcasted_iota(jnp.int32, (EXPERTS, 1, 1), 0)
+    named = routes.T[None] == ids
+    hit = named.any(axis=1)
+    share = jnp.where(named, route_weights.T.astype(F32)[None], 0.0).sum(axis=1)
+    before = (
+        lax.broadcasted_iota(jnp.int32, (count, count), 0)
+        < lax.broadcasted_iota(jnp.int32, (count, count), 1)
+    )
+    rank = jnp.dot(hit.astype(BF), before.astype(BF), preferred_element_type=F32)
+    slot = jnp.where(hit, rank, -1.0)
+    meta = jnp.concatenate(
+        [slot[:, None], share[:, None], jnp.zeros((EXPERTS, 6, count), F32)], axis=1)
+    dma = pltpu.SemaphoreType.DMA
+    vmem = pltpu.VMEM
+    any_spec = pl.BlockSpec(memory_space=pl.ANY)
+    vmem_spec = pl.BlockSpec(memory_space=pltpu.VMEM)
+    return pl.pallas_call(
+        functools.partial(kernel, nt, nq),
+        out_shape=jax.ShapeDtypeStruct((count, local_width), BF),
+        in_specs=[any_spec, vmem_spec, any_spec, any_spec, any_spec],
+        out_specs=vmem_spec,
+        scratch_shapes=[
+            vmem((n, ROLES, count, kc), BF),
+            vmem((rows, kc), BF),
+            vmem((rows, hidden), F32),
+            vmem((rows, hidden), F32),
+            vmem((rows, hidden), BF),
+            vmem((W_SLOTS, kc, hidden), BF),
+            vmem((W_SLOTS, kc, hidden), BF),
+            vmem((D_SLOTS, hidden, kc), BF),
+            vmem((rows, ROLES * count), BF),
+            vmem((ROLES * count, rows), BF),
+            vmem((ROLES, 8, count), F32),
+            vmem((K_SLOTS, 2 * count, kc), F32),
+            vmem((n, 2 * count, kc), BF),
+            vmem((n, 2 * count, kc), BF),
+            vmem((n, count, kc), BF),
+            vmem((n, count, kc), BF),
+            vmem((n, count, kc), BF),
+            vmem((n, count, kc), BF),
+            dma((nq,)), dma((2, W_SLOTS)), dma((D_SLOTS,)), dma((ROLES,)), dma((ROLES,)),
+            dma(((nt - 1) * nq,)), dma((n,)), dma((n,)), dma((n,)), dma((n,)), dma((n,)),
+            dma((n,)), dma((n,)), dma((n,)), dma((n,)), dma((n,)), dma((n,)), dma((n,)), dma((n,)),
+        ],
+        compiler_params=pltpu.CompilerParams(
+            collective_id=0, has_side_effects=True, vmem_limit_bytes=62 * 1024 * 1024),
+        cost_estimate=pl.CostEstimate(
+            flops=6 * rows * hidden * local_width * nt,
+            bytes_accessed=6 * hidden * local_width * nt, transcendentals=rows * hidden),
+    )(tokens, meta, gate_weight, up_weight, down_weight)
 
 def assign(flat, targets, capacity):
     hit = (flat[:, None, :] == targets[:, :, None]).astype(jnp.int32)
@@ -80,6 +427,8 @@
         P(("expert", "tensor"), None),
     )
     out_specs = P(("groups", "expert"), "tensor")
+    small = mesh.shape["expert"] == EXPERTS and mesh.shape["tensor"] > 1
+    body = functools.partial(fused, mesh) if small else per_device
     return jax.shard_map(
-        per_device, mesh=mesh, in_specs=in_specs, out_specs=out_specs, check_vma=False
-    )
+        body, mesh=mesh, in_specs=in_specs, out_specs=out_specs, check_vma=False
+    )

time: 234 us -> 115 us (0.49)
  waiting for transfers between devices: 116 us -> 0 us
  Pallas kernels: 0 us -> 110 us
  blocking collectives: 43.7 us -> 0 us
  matrix products: 41.6 us -> 0.13 us
  between operations: 13.5 us -> 0.01 us
  local copies, waits for them, and re-layouts: 9.77 us -> 1.85 us
  starting transfers between devices: 3.72 us -> 0 us
  other arithmetic: 5.34 us -> 2.72 us
    pallas_call x0 -> x1, Pallas kernels: none -> 110 us  [fused(): pl.pallas_call(functools.partial(kernel, nt, nq), out_shape=jax.ShapeDtyp...]
    reduce_scatter x1 -> x0, waiting for transfers between devices: 64.5 us -> none  [per_device(): lax.psum_scatter(lax.dot_general(down_weight, hidden, (((0,), (1,)), ((),...]
    all_to_all x1 -> x0, blocking collectives: 43.7 us -> none  [per_device(): lax.all_to_all(outgoing, 'expert', split_axis=0, concat_axis=0, tiled=True)]
    dot_general x5 -> x1, matrix products: 41.6 us -> 0.13 us  [fused(): jnp.dot(hit.astype(BF), before.astype(BF), preferred_element_type=F32)]
    all_gather x1 -> x0, waiting for transfers between devices: 38.7 us -> none  [per_device(): features = lax.all_gather(tokens, 'tensor', axis=1, tiled=True)]
    all_to_all x1 -> x0, waiting for transfers between devices: 12.2 us -> none  [per_device(): lax.all_to_all(partial_rows.astype(jnp.bfloat16), 'expert', split_axis=1,...]
    reshape x2 -> x0, local copies, waits for them, and re-layouts: 4.8 us -> none  [the longest x1 2.72 us: per_device(): doubled = jnp.repeat(features, TOP, axis=0)]
    all_to_all x1 -> x0, starting transfers between devices: 3.68 us -> none  [per_device(): lax.all_to_all(partial_rows.astype(jnp.bfloat16), 'expert', split_axis=1,...]
  transfers between devices with their start and end apart: 3 -> 0, of which waited for: 3 -> 0; matrix products, arithmetic and copies ran while one was open for 1% -> 0% of each run, Pallas kernels for 0% -> 0%
where the time goes in v1:
time: 115 us
  Pallas kernels  110 us (96%)
  other arithmetic  2.72 us (2%)
  local copies, waits for them, and re-layouts  1.85 us (2%)
    pallas_call x1, Pallas kernels, fused(): pl.pallas_call(functools.partial(kernel, nt, nq), out_shape=jax.ShapeDtyp...  110 us

profile of v1, /device:TPU:0, one launch (start us, length us, event | category | flops | bytes accessed | tf_op | source)
XLA Modules:
  0.0 114.7 jit_solution(16514327031663016393)
XLA Ops:
  0.0 0.7 fusion
  0.7 0.1 pad.2.clone
  0.8 0.7 convert_bitcast_fusion
  1.4 0.7 select_reduce_fusion
  2.1 0.1 convolution_select_fusion
  2.3 0.7 maximum_maximum_fusion.meta
  2.9 110.0 %shard_map.64 = bf16[128,1536]{1,0:T(8,128)(2,1)} custom-call(bf16[128,1536]{1,0:T(8,128)(2,1)} %tok.1, f32[4,8,128]{2,1,0:T(8,128)} %maximum_maximum_fusion.meta, bf16[6144,2048]{1,0:T(8,128)(2,1)} %wg.1, bf16[6144,2048]{1,0:T(8,128)(2,1)} %wu.1, bf16[2048,6144]{1,0:T(8,128)(2,1)} %wd.1), custom_call_target="tpu_custom_call" | custom-call | flops 21743271936 | bytes 75497472 | tf_op jit(solution)/shard_map/pallas_call | solution.py:323
  112.9 1.8 %copy.8 = bf16[128,1536]{1,0:T(8,128)(2,1)} copy(bf16[128,1536]{1,0:T(8,128)(2,1)} %shard_map.64) | data formatting | bytes 786432
  (1 shorter events, 0.0 us)

commit v2 on v1

--- a/solution.py
+++ b/solution.py
@@ -14,7 +14,11 @@
 F32 = jnp.float32
 W_SLOTS = 3
 D_SLOTS = 3
-K_SLOTS = 4
+K_SLOTS = 6
+FWD_LAG = 2
+DOT_LAG = 3
+X_LAG = 2
+Z_LAG = 4
 ROLES = 4
 
 
@@ -173,15 +177,15 @@
                 x_copy(k).start()
                 own_copy(k).start()
 
-        @pl.when((i >= 1) & (i < n + 1))
-        def _():
-            k = in_chunk(i - 1)
+        @pl.when((i >= FWD_LAG) & (i < n + FWD_LAG))
+        def _():
+            k = in_chunk(i - FWD_LAG)
             x_copy(k).wait_recv()
             fwd_copy(k).start()
 
-        @pl.when(i >= 2)
-        def _():
-            j = i - 2
+        @pl.when(i >= DOT_LAG)
+        def _():
+            j = i - DOT_LAG
             k = in_chunk(j)
             s = lax.rem(j, W_SLOTS)
             own_copy(k).wait_recv()
@@ -208,7 +212,7 @@
 
         return carry
 
-    lax.fori_loop(0, n + 2, gather_step, 0)
+    lax.fori_loop(0, n + DOT_LAG, gather_step, 0)
 
     def activate(t, carry):
         cols = pl.ds(pl.multiple_of(t * tile, tile), tile)
@@ -217,7 +221,7 @@
 
     lax.fori_loop(0, gbuf.shape[2] // tile, activate, 0)
 
-    width = 256
+    width = kc
 
     def return_step(i, carry):
         @pl.when(i < n)
@@ -242,17 +246,17 @@
             def _():
                 d_copy(i + D_SLOTS, out_chunk(i + D_SLOTS)).start()
 
-        @pl.when((i >= 1) & (i < n + 1))
-        def _():
-            k = out_chunk(i - 1)
-            ks = lax.rem(i - 1, K_SLOTS)
+        @pl.when((i >= X_LAG) & (i < n + X_LAG))
+        def _():
+            k = out_chunk(i - X_LAG)
+            ks = lax.rem(i - X_LAG, K_SLOTS)
             rsib_copy(k).wait_recv()
             x_out[k] = (keep[ks, tokens:] + sib_in[k, tokens:].astype(F32)).astype(BF)
             rx_copy(k).start()
 
-        @pl.when(i >= 2)
-        def _():
-            j = i - 2
+        @pl.when(i >= Z_LAG)
+        def _():
+            j = i - Z_LAG
             k = out_chunk(j)
             ks = lax.rem(j, K_SLOTS)
             rx_copy(k).wait_recv()
@@ -266,7 +270,7 @@
 
         return carry
 
-    lax.fori_loop(0, n + 2, return_step, 0)
+    lax.fori_loop(0, n + Z_LAG, return_step, 0)
 
     for q in range(nq):
         total = z_out[z * nq + q].astype(F32)

time: 115 us -> 110 us (0.957)
  Pallas kernels: 110 us -> 104 us
    pallas_call x1, Pallas kernels: 110 us -> 104 us  [fused(): pl.pallas_call(functools.partial(kernel, nt, nq), out_shape=jax.ShapeDtyp...]
where the time goes in v2:
time: 110 us; the launch traced here: 109 us
  Pallas kernels  104 us (95%)
  other arithmetic  2.72 us (2%)
  local copies, waits for them, and re-layouts  1.85 us (2%)
    pallas_call x1, Pallas kernels, fused(): pl.pallas_call(functools.partial(kernel, nt, nq), out_shape=jax.ShapeDtyp...  104 us

profile of v2, /device:TPU:0, one launch (start us, length us, event | category | flops | bytes accessed | tf_op | source)
XLA Modules:
  0.0 109.0 jit_solution(9696009151970872782)
XLA Ops:
  0.0 0.7 fusion
  0.7 0.1 pad.2.clone
  0.8 0.7 convert_bitcast_fusion
  1.4 0.7 select_reduce_fusion
  2.1 0.1 convolution_select_fusion
  2.3 0.7 maximum_maximum_fusion.meta
  2.9 104.3 %shard_map.64 = bf16[128,1536]{1,0:T(8,128)(2,1)} custom-call(bf16[128,1536]{1,0:T(8,128)(2,1)} %tok.1, f32[4,8,128]{2,1,0:T(8,128)} %maximum_maximum_fusion.meta, bf16[6144,2048]{1,0:T(8,128)(2,1)} %wg.1, bf16[6144,2048]{1,0:T(8,128)(2,1)} %wu.1, bf16[2048,6144]{1,0:T(8,128)(2,1)} %wd.1), custom_call_target="tpu_custom_call" | custom-call | flops 21743271936 | bytes 75497472 | tf_op jit(solution)/shard_map/pallas_call | solution.py:327
  107.3 1.8 %copy.8 = bf16[128,1536]{1,0:T(8,128)(2,1)} copy(bf16[128,1536]{1,0:T(8,128)(2,1)} %shard_map.64) | data formatting | bytes 786432
  (1 shorter events, 0.0 us)
